TPU v7x, 256 devices: a whole 4x4x8 slice. The times are simulated.
256 devices in a mesh: replica: 32 (over z, y_lo, core), fsdp: 8 (over y_hi, x).
Axes of the slice: x: 4, y: 4 (y_hi: 2, y_lo: 2; y = y_hi * 2 + y_lo), z: 8, core: 2. Of those that a mesh axis runs over, the one named last changes fastest.
Arguments:
- inputs: bfloat16 [32, 2048, 2560], P('replica', 'fsdp'), may hold values from -6 to 6
- targets: bfloat16 [32, 2048, 2560], P('replica', 'fsdp'), may hold values from -6 to 6
- masked: int32 [32, 2048], P('replica', 'fsdp'), may hold values 0 or 1
- step_index: int32 [], replicated, may hold values from 0 to 999
- weights: float32 [32, 2560, 2560], P('replica', 'fsdp'), may hold values from -0.125 to 0.125
- momentum: bfloat16 [32, 2560, 2560], P('replica', 'fsdp'), may hold values from -0.119628906 to 0.119628906
Outputs:
- new_weights: float32 [32, 2560, 2560], P('replica', 'fsdp')
- new_momentum: bfloat16 [32, 2560, 2560], P('replica', 'fsdp')
All inputs are finite; a program needn't handle non-finite values. No bound on the sum of `masked` on one device may be relied on, other than what follows from the above.
Results may differ from a plain program's by a relative error of at most 0.015.
Values may be sent and summed in bfloat16 or wider, within the bound.
A program may use at most 128 MiB of HBM per device.

v0:
```python
from functools import partial

import jax
import jax.numpy as jnp
from jax import lax
from jax.sharding import PartitionSpec as P


def shortened(x):

    def short(part):
        return part.astype(jnp.bfloat16) if part.dtype == jnp.float32 else part

    return jax.tree.map(short, x)


def passed_along(x, axis, by):
    length = lax.axis_size(axis)
    return lax.ppermute(x, axis, [(i, (i + by) % length) for i in range(length)])


def mix_sequential(near, later, shard):
    moved = jax.tree.map(
        lambda part, own: part.astype(own.dtype),
        passed_along(shortened(shard), "replica", near),
        shard,
    )
    half = (shard + moved) / 2.0
    moved_again = passed_along(shortened(half), "replica", later).astype(half.dtype)
    return (half + moved_again) / 2.0


def local(inputs, targets, masked, step_index, weights, momentum):
    tokens = inputs[0]
    goals = targets[0]
    marks = masked[0]
    shard = weights[0]
    seq_len = tokens.shape[0] * lax.axis_size("fsdp")
    columns = tokens
    pred = jnp.dot(
        columns,
        lax.all_gather(shard.astype(jnp.bfloat16), "fsdp", axis=0, tiled=True),
        preferred_element_type=jnp.float32,
    )
    scale = marks.astype(jnp.float32)[:, None] / seq_len
    resid = (scale * (pred - goals.astype(jnp.float32))).astype(jnp.bfloat16)
    columns = tokens
    grad = lax.psum_scatter(
        lax.dot_general(
            columns, resid, (((0,), (0,)), ((), ())), preferred_element_type=jnp.float32
        ).astype(jnp.bfloat16),
        "fsdp",
        scatter_dimension=0,
        tiled=True,
    ).astype(jnp.float32)
    new_momentum = (0.9 * momentum[0].astype(jnp.float32) + grad).astype(jnp.bfloat16)
    count = lax.axis_size("replica")
    levels = count.bit_length() - 1
    branches = [
        partial(mix_sequential, 2**level, 2 ** ((level + 1) % levels)) for level in range(levels)
    ]
    mixed = lax.switch(step_index % levels, branches, shard)
    rate = (step_index.astype(jnp.float32) + 1.0) / 500.0
    new_weights = mixed - rate * new_momentum.astype(jnp.float32)
    return (new_weights[None], new_momentum[None])


def solution(mesh):
    in_specs = (
        P("replica", "fsdp", None),
        P("replica", "fsdp", None),
        P("replica", "fsdp"),
        P(),
        P("replica", "fsdp", None),
        P("replica", "fsdp", None),
    )
    out_specs = (P("replica", "fsdp", None), P("replica", "fsdp", None))
    return jax.shard_map(local, mesh=mesh, in_specs=in_specs, out_specs=out_specs, check_vma=False)
```

profile of v0, /device:TPU:1, one launch (start us, length us, event | category | flops | bytes accessed | tf_op | source)
XLA Modules:
  0.0 388.5 jit_solution(1329381944244153886)
XLA Ops:
  7.2 0.0 copy-start
  7.2 0.0 all-gather.2.cloned.1.call-start
  7.2 3.4 bitcast_convert_fusion
  10.7 0.0 all-gather.2.cloned.1.call-update
  10.7 0.0 reduce-scatter.4.cloned.1.call-start
  10.8 161.2 %all-gather.2.cloned.1.call-done = bf16[2560,2560]{1,0:T(8,128)(2,1)} async-done(((bf16[320,2560]{1,0:T(8,128)(2,1)}), bf16[2560,2560]{1,0:T(8,128)(2,1)}) %all-gather.2.cloned.1.call-update) | async-done | bytes 13107216 | tf_op jit(solution)/shard_map/all_gather | solution.py:42
  172.0 14.0 %fusion.5 = bf16[2560,2560]{0,1:T(8,128)(2,1)} fusion(bf16[2560,2560]{1,0:T(8,128)(2,1)} %all-gather.2.cloned.1.call-done, bf16[1,256,2560]{2,1,0:T(8,128)(2,1)S(1)} %copy-done.9, bf16[1,256,2560]{2,1,0:T(8,128)(2,1)S(1)} %copy-done, f32[256]{0:T(256)S(1)} %bitcast.34), kind=kOutput, calls=%fused_computation.16 | convolution fusion | flops 6720061440 | bytes 28836864 | tf_op jit(solution)/shard_map/dot_general | solution.py:49
  186.0 17.7 %copy.16 = bf16[2560,2560]{1,0:T(8,128)(2,1)} copy(bf16[2560,2560]{0,1:T(8,128)(2,1)} %fusion.5) | data formatting | bytes 26214400
  203.6 0.0 reduce-scatter.4.cloned.1.call-update
  204.3 3.6 copy.12
  207.9 123.1 %conditional.1 = (f32[320,2560]{0,1:T(8,128)}) conditional(s32[]{:T(128)} %clamp.3, f32[320,2560]{1,0:T(8,128)} %bitcast.29, f32[320,2560]{1,0:T(8,128)} %bitcast.30, f32[320,2560]{1,0:T(8,128)} %bitcast.31, f32[320,2560]{1,0:T(8,128)} %bitcast.32, f32[320,2560]{1,0:T(8,128)} %bitcast.33), branch_computations={%region_0.0_spmd, %region_1.2_spmd, %region_2.3_spmd, %region_3.4_... | conditional | flops 9011200 | bytes 54067316 | solution.py:62
  208.0 2.2 convert_element_type.78
  210.2 1.4 collective-permute-start.4
  211.6 36.9 %collective-permute-done.4 = bf16[320,2560]{1,0:T(8,128)(2,1)S(1)} collective-permute-done((bf16[320,2560]{1,0:T(8,128)(2,1)S(1)}, bf16[320,2560]{1,0:T(8,128)(2,1)S(1)}, u32[]{:S(2)}, u32[]{:S(2)}) %collective-permute-start.4) | collective-permute-done | bytes 1638432 | tf_op jit(solution)/shard_map/cond/branch_2_fun/ppermute | solution.py:19
  248.5 0.5 fusion.2
  249.0 0.5 collective-permute-start.5
  249.4 73.8 %collective-permute-done.5 = bf16[320,2560]{1,0:T(8,128)(2,1)S(1)} collective-permute-done((bf16[320,2560]{1,0:T(8,128)(2,1)S(1)}, bf16[320,2560]{1,0:T(8,128)(2,1)S(1)}, u32[]{:S(2)}, u32[]{:S(2)}) %collective-permute-start.5) | collective-permute-done | bytes 1638432 | tf_op jit(solution)/shard_map/cond/branch_2_fun/ppermute | solution.py:19
  323.2 2.4 add_multiply_fusion.4
  325.6 5.5 %copy.20 = f32[320,2560]{0,1:T(8,128)} copy(f32[320,2560]{1,0:T(8,128)} %add_multiply_fusion.4) | data formatting | bytes 6553600 | tf_op jit(solution)/shard_map/cond | solution.py:62
  331.1 32.2 %reduce-scatter.4.cloned.1.call-done = bf16[320,2560]{1,0:T(8,128)(2,1)} async-done(((bf16[2560,2560]{1,0:T(8,128)(2,1)}), bf16[320,2560]{1,0:T(8,128)(2,1)}) %reduce-scatter.4.cloned.1.call-update) | async-done | bytes 1638416
  363.2 3.8 copy.17
  367.1 6.0 %fusion.13 = (bf16[1,320,2560]{1,2,0:T(8,128)(2,1)}, f32[1,320,2560]{1,2,0:T(8,128)}) fusion(bf16[320,2560]{0,1:T(8,128)(2,1)} %copy.17, bf16[1,320,2560]{1,2,0:T(8,128)(2,1)S(1)} %copy.12, f32[320,2560]{0,1:T(8,128)} %get-tuple-element.17, f32[]{:T(128)S(6)} %div.41), kind=kLoop, calls=%fused_computation.26 | loop fusion | flops 6553600 | bytes 11468804 | tf_op jit(solution)/shard_map/broadcast_in_dim | solution.py:65
  373.1 5.4 %copy.14 = f32[1,320,2560]{2,1,0:T(8,128)} copy(f32[1,320,2560]{1,2,0:T(8,128)} %get-tuple-element.19) | data formatting | bytes 6553600
  378.5 3.2 copy.15
  (12 shorter events, 0.0 us)
Async XLA Ops:
  7.2 164.8 %copy-start = (bf16[1,256,2560]{2,1,0:T(8,128)(2,1)S(1)}, bf16[1,256,2560]{2,1,0:T(8,128)(2,1)}, u32[]{:S(2)}) copy-start(bf16[1,256,2560]{2,1,0:T(8,128)(2,1)} %param.11) | copy-start | bytes 3932164
  7.2 3.6 copy-start.8
  7.2 164.8 %copy-start.9 = (bf16[1,256,2560]{2,1,0:T(8,128)(2,1)S(1)}, bf16[1,256,2560]{2,1,0:T(8,128)(2,1)}, u32[]{:S(2)}) copy-start(bf16[1,256,2560]{2,1,0:T(8,128)(2,1)} %param.12) | copy-start | bytes 3932164
  7.2 164.8 %all-gather.2.cloned.1.call-start = ((), (), s32[]{:S(2)}) async-start(), calls=%async_computation.1 | async-start | bytes 14745600 | tf_op jit(solution)/shard_map/all_gather | solution.py:42
  10.7 352.6 %reduce-scatter.4.cloned.1.call-start = ((), (), s32[]{:S(2)}) async-start(), calls=%async_computation.2 | async-start | bytes 14745600
  208.0 40.5 %copy-start.4 = (f32[320,2560]{1,0:T(8,128)S(1)}, f32[320,2560]{1,0:T(8,128)}, u32[]{:S(2)}) copy-start(f32[320,2560]{1,0:T(8,128)} %param.2) | copy-start | bytes 9830404 | tf_op jit(solution)/shard_map/cond
  210.2 38.3 %collective-permute-start.4 = (bf16[320,2560]{1,0:T(8,128)(2,1)S(1)}, bf16[320,2560]{1,0:T(8,128)(2,1)S(1)}, u32[]{:S(2)}, u32[]{:S(2)}) collective-permute-start(bf16[320,2560]{1,0:T(8,128)(2,1)S(1)} %convert_element_type.78), channel_id=1, source_target_pairs={{0,32},{8,40},{16,48},{24,56},{32,64},{40,72},{48,80},{56,88},{64,... | collective-permute-start | bytes 4915208 | tf_op jit(solution)/shard_map/cond/branch_2_fun/ppermute | solution.py:19
  249.0 74.2 %collective-permute-start.5 = (bf16[320,2560]{1,0:T(8,128)(2,1)S(1)}, bf16[320,2560]{1,0:T(8,128)(2,1)S(1)}, u32[]{:S(2)}, u32[]{:S(2)}) collective-permute-start(bf16[320,2560]{1,0:T(8,128)(2,1)S(1)} %fusion.2), channel_id=1, source_target_pairs={{0,64},{8,72},{16,80},{24,88},{32,96},{40,104},{48,112},{56,120},{... | collective-permute-start | bytes 4915208 | tf_op jit(solution)/shard_map/cond/branch_2_fun/ppermute | solution.py:19
  373.1 5.4 %copy-start.7 = (bf16[1,320,2560]{1,2,0:T(8,128)(2,1)S(1)}, bf16[1,320,2560]{1,2,0:T(8,128)(2,1)}, u32[]{:S(2)}) copy-start(bf16[1,320,2560]{1,2,0:T(8,128)(2,1)} %get-tuple-element.18) | copy-start | bytes 4915204
  373.1 8.6 %copy-start.1 = (bf16[1,256,2560]{2,1,0:T(8,128)(2,1)S(1)}, bf16[1,256,2560]{2,1,0:T(8,128)(2,1)}, u32[]{:S(2)}) copy-start(bf16[1,256,2560]{2,1,0:T(8,128)(2,1)} %param.11) | copy-start | bytes 3932164
Sparse Core Ops, SparseCore 0:
  11.2 160.7 all-gather.1
  203.8 159.4 reduce-scatter.3
where the time goes:
time: 389 us
  waiting for transfers between devices  304 us (78%)
  local copies, waits for them, and re-layouts  39.2 us (10%)
  between operations  14.8 us (4%)
  other arithmetic  14.5 us (4%)
  matrix products  14 us (4%)
    all_gather x1, waiting for transfers between devices, local(): lax.all_gather(shard.astype(jnp.bfloat16), 'fsdp', axis=0, tiled=True)  161 us
    ppermute x2, waiting for transfers between devices, passed_along(): lax.ppermute(x, axis, [(i, (i + by) % length) for i in range(length)])  111 us
    unnamed x15, local copies, waits for them, and re-layouts  33.7 us
    unnamed x3, waiting for transfers between devices  32.2 us
    dot_general x1, matrix products, local(): lax.dot_general(columns, resid, (((0,), (0,)), ((), ())), preferred_eleme...  14 us
  transfers between devices with their start and end apart: 4, of which 4 were waited for; matrix products, arithmetic and copies ran while one was open for 4% of the time, Pallas kernels for 0%

commit v1 on v0

v1 whole, which is shorter than its diff:
```python
import functools

import jax
import jax.numpy as jnp
from jax import lax
from jax.experimental import pallas as pl
from jax.experimental.pallas import tpu as pltpu
from jax.sharding import PartitionSpec as P

MESH = pl.DeviceIdType.MESH
BF = jnp.bfloat16
F32 = jnp.float32
COLS = 256
NT = 10
NJ = 5
ROWS = 320
SEQ = 256
HALF = 1280


def kernel(level, rate_ref, x_hbm, t_hbm, m_hbm, w_hbm, mom_hbm, neww_hbm, newm_hbm,
           win, wb, mom, xk, xt, tk, mk, wk, ps, pr, rb, gb, go, gr, hs, gh, ga, hb, gbuf,
           ld, xs, xr, xos, xor_, ts, tr, ms, mr, ws, wr, wss, wsr, pss, psr, rs, rr,
           gs, grr, hss, hsr, as_, ar, bs, br, outs):
    r = lax.axis_index("replica")
    f = lax.axis_index("fsdp")
    c = lax.rem(r, 2)
    pair = r - c
    yh = f // 4
    x = lax.rem(f, 4)
    lo = lax.rem(x, 2)
    hi = x // 2
    xo = x + 1 - 2 * lo
    xs_ = 3 - x
    o = lax.rem(lo + hi, 2)
    home = c == yh

    def dev(core, y, xx):
        return (pair + core, y * 4 + xx)

    def other(offset):
        return (lax.rem(r + offset, 32), f)

    def remote(src, dst, ss, rsem, to):
        return pltpu.make_async_remote_copy(src_ref=src, dst_ref=dst, send_sem=ss, recv_sem=rsem,
                                            device_id=to, device_id_type=MESH)

    def arrived(dst, rsem):
        remote(dst, dst, rsem, rsem, dev(1 - c, yh, x)).wait_recv()

    w_loads = [pltpu.make_async_copy(w_hbm.at[:, pl.ds(t * COLS, COLS)], win.at[t], ld.at[t]) for t in range(NT)]
    for copy in w_loads:
        copy.start()
    m_load = pltpu.make_async_copy(mom_hbm, mom, ld.at[NT])
    m_load.start()

    near, later = 2**level, 2 ** ((level + 1) % 5)
    if level == 3:
        offsets = [8, 16, 24]
    else:
        offsets = sorted({near, 32 - near, later, 32 - later})
    barrier = pltpu.get_barrier_semaphore()
    peers = [dev(1 - c, yh, x), dev(c, 1 - yh, x), dev(1 - c, 1 - yh, x), dev(c, yh, xs_)]
    peers += [dev(a, b, xo) for a in (0, 1) for b in (0, 1)]
    peers += [other(a) for a in offsets]
    for peer in peers:
        pl.semaphore_signal(barrier, inc=1, device_id=peer, device_id_type=MESH)
    pl.semaphore_wait(barrier, len(peers))

    x_to = xk.at[yh * 2 + lo]
    x_away = []
    for k in range(2):
        src = x_hbm.at[:, pl.ds(k * HALF, HALF)]
        mine = jnp.logical_and(home, c == k)
        x_away.append((jnp.logical_not(mine), remote(src, x_to, xs.at[k], xr.at[yh], dev(k, c, x))))

        @pl.when(mine)
        def _(src=src):
            pltpu.make_async_copy(src, x_to, xr.at[yh]).start()

        @pl.when(jnp.logical_not(mine))
        def _(copy=x_away[-1][1]):
            copy.start()

    def send_w(j):
        keep = wb.at[o * NJ + j]
        give = wb.at[(1 - o) * NJ + j]
        dst = wk.at[j, pl.ds(pl.multiple_of(x * ROWS, ROWS), ROWS)]
        first = remote(keep, dst, ws.at[0, j], wr.at[lo, j], dev(yh, c, x))
        second = remote(give, dst, ws.at[1, j], wr.at[lo, j], dev(yh, c, xo))
        return keep, dst, first, second

    for t in range(NT):
        w_loads[t].wait()
        wb[t] = win[t].astype(BF)

    for j in range(NJ):
        keep, dst, first, second = send_w(j)

        @pl.when(home)
        def _(keep=keep, dst=dst, j=j):
            pltpu.make_async_copy(keep, dst, wr.at[lo, j]).start()

        @pl.when(jnp.logical_not(home))
        def _(first=first):
            first.start()

        second.start()

    if level == 3:
        member = r // 8
        quarter = ROWS // 4

        def part(q):
            return pl.ds(pl.multiple_of(q * quarter, 16), quarter)

        a_copies = []
        for d in range(1, 4):
            q = lax.rem(member + d, 4)
            a_copies.append(remote(wb.at[:, part(q)], ga.at[:, pl.ds((d - 1) * quarter, quarter)],
                                   as_.at[d - 1], ar.at[d - 1], other(8 * d)))
    else:
        a_copies = [remote(wb.at[t], ga.at[t], as_.at[t], ar.at[t], other(near)) for t in range(NT)]
    for copy in a_copies:
        copy.start()

    t_cols = [pl.ds(pl.multiple_of(h * HALF, HALF), HALF) for h in (o, 1 - o)]
    t_dst = tk.at[pl.ds(pl.multiple_of(lo * SEQ, SEQ), SEQ)]
    m_dst = mk.at[pl.ds(pl.multiple_of(lo * SEQ, SEQ), SEQ)]
    t_first = remote(t_hbm.at[:, t_cols[0]], t_dst, ts.at[0], tr.at[lo], dev(yh, c, x))
    t_second = remote(t_hbm.at[:, t_cols[1]], t_dst, ts.at[1], tr.at[lo], dev(yh, c, xo))
    m_first = remote(m_hbm, m_dst, ms.at[0], mr.at[lo], dev(yh, c, x))
    m_second = remote(m_hbm, m_dst, ms.at[1], mr.at[lo], dev(yh, c, xo))

    @pl.when(home)
    def _():
        pltpu.make_async_copy(t_hbm.at[:, t_cols[0]], t_dst, tr.at[lo]).start()
        pltpu.make_async_copy(m_hbm, m_dst, mr.at[lo]).start()

    @pl.when(jnp.logical_not(home))
    def _():
        t_first.start()
        m_first.start()

    t_second.start()
    m_second.start()

    def turn(slot):
        xt[slot] = xk[slot].T

    relays = []
    for step in range(2):
        ry = yh if step == 0 else 1 - yh
        slot = ry * 2 + lo
        arrived(xk.at[slot], xr.at[ry])
        copy = remote(xk.at[slot], xk.at[slot], xos.at[step], xor_.at[ry], dev(c, yh, xo))
        copy.start()
        relays.append(copy)
        turn(slot)

    mine_rows = pl.ds(pl.multiple_of(hi * 2 * ROWS, 2 * ROWS), 2 * ROWS)
    their_rows = pl.ds(pl.multiple_of((1 - hi) * 2 * ROWS, 2 * ROWS), 2 * ROWS)
    w_on = []
    for j in range(NJ):
        for side in range(2):
            arrived(wk.at[j, pl.ds(pl.multiple_of(hi * 2 * ROWS, 2 * ROWS) + side * ROWS, ROWS)], wr.at[side, j])
        copy = remote(wk.at[j, mine_rows], wk.at[j, mine_rows], wss.at[j], wsr.at[j], dev(c, yh, xs_))
        copy.start()
        w_on.append(copy)

    for step in range(2):
        ry = yh if step == 0 else 1 - yh
        slot = ry * 2 + (1 - lo)
        arrived(xk.at[slot], xor_.at[ry])
        turn(slot)

    core = dev(1 - c, yh, x)
    half_rows = [pl.ds(pl.multiple_of(h * 512, 512), 512) for h in (c, 1 - c)]
    p_copies, r_copies, g_copies, h_copies = [], [], [], []

    def step_p(j):
        arrived(wk.at[j, their_rows], wsr.at[j])

        def one(ry):
            @pl.loop(0, 2)
            def _(side):
                b = ry * 2 + side
                rows = pl.ds(pl.multiple_of(b * SEQ, SEQ), SEQ)
                ps[j, rows] = jnp.dot(xk[b], wk[j], preferred_element_type=F32)

        one(1 - c)
        copy = remote(ps.at[j, half_rows[1]], pr.at[j], pss.at[j], psr.at[j], core)
        copy.start()
        p_copies.append(copy)
        one(c)

    def step_r(j):
        if j == 0:
            for side in range(2):
                arrived(tk.at[pl.ds(side * SEQ, SEQ)], tr.at[side])
                arrived(mk.at[pl.ds(side * SEQ, SEQ)], mr.at[side])
        arrived(pr.at[j], psr.at[j])

        @pl.loop(0, 8)
        def _(i):
            rows = pl.ds(pl.multiple_of(i * 64, 64), 64)
            full = pl.ds(pl.multiple_of(c * 512 + i * 64, 64), 64)
            scale = mk[rows].astype(F32)
            scale = jnp.concatenate([scale, scale], axis=1)
            pred = ps[j, full] + pr[j, rows]
            goal = tk[rows, pl.ds(j * COLS, COLS)].astype(F32)
            rb[j, full] = (scale * (pred - goal)).astype(BF)

        copy = remote(rb.at[j, half_rows[0]], rb.at[j, half_rows[0]], rs.at[j], rr.at[j], core)
        copy.start()
        r_copies.append(copy)

    def product(j, row):
        total = None
        for b in range(4):
            term = jnp.dot(xt[b, pl.ds(pl.multiple_of(row, ROWS), ROWS)], rb[j, pl.ds(b * SEQ, SEQ)],
                           preferred_element_type=F32)
            total = term if total is None else total + term
        return total

    def step_g(j):
        arrived(rb.at[j, half_rows[1]], rr.at[j])

        @pl.loop(0, 2)
        def _(i):
            gb[j, pl.ds(pl.multiple_of(i * ROWS, ROWS), ROWS)] = product(j, ((1 - hi) * 2 + i) * ROWS).astype(BF)

        copy = remote(gb.at[j], gr.at[j], gs.at[j], grr.at[j], dev(c, yh, xs_))
        copy.start()
        g_copies.append(copy)

        @pl.loop(0, 2)
        def _(i):
            go[j, pl.ds(pl.multiple_of(i * ROWS, ROWS), ROWS)] = product(j, (hi * 2 + i) * ROWS)

    def step_h(j):
        arrived(gr.at[j], grr.at[j])

        def one(side):
            @pl.loop(0, 5)
            def _(i):
                rows = pl.ds(pl.multiple_of(side * ROWS + i * 64, 64), 64)
                hs[j, rows] = (go[j, rows] + gr[j, rows].astype(F32)).astype(BF)
            return hs.at[j, pl.ds(pl.multiple_of(side * ROWS, ROWS), ROWS)]

        dst = gh.at[o * NJ + j]
        sem = hsr.at[o * NJ + j]
        copy = remote(one(1 - lo), dst, hss.at[1, j], sem, dev(yh, c, xo))
        copy.start()
        own = one(lo)
        first = remote(own, dst, hss.at[0, j], sem, dev(yh, c, x))
        h_copies.append((first, copy))

        @pl.when(home)
        def _():
            pltpu.make_async_copy(own, dst, sem).start()

        @pl.when(jnp.logical_not(home))
        def _():
            first.start()

    b_copies = []

    def gossip_half(t):
        arrived(ga.at[t], ar.at[t])

        @pl.loop(0, 5)
        def _(i):
            rows = pl.ds(pl.multiple_of(i * 64, 64), 64)
            half = (win[t, rows] + ga[t, rows].astype(F32)) * 0.5
            win[t, rows] = half
            hb[t, rows] = half.astype(BF)

        copy = remote(hb.at[t], gbuf.at[t], bs.at[t], br.at[t], other(later))
        copy.start()
        b_copies.append(copy)

    def gossip_quarter():
        for d in range(3):
            arrived(ga.at[:, pl.ds(d * quarter, quarter)], ar.at[d])

        @pl.loop(0, NT)
        def _(t):
            total = win[t, part(member)]
            for d in range(3):
                total += ga[t, pl.ds(d * quarter, quarter)].astype(F32)
            hb[t, part(member)] = (total * 0.25).astype(BF)

        for d in range(1, 4):
            copy = remote(hb.at[:, part(member)], hb.at[:, part(member)], bs.at[d - 1], br.at[d - 1], other(8 * d))
            copy.start()
            b_copies.append(copy)

    for j in range(NJ + 3):
        if j < NJ:
            step_p(j)
        if 1 <= j < NJ + 1:
            step_r(j - 1)
        if 2 <= j < NJ + 2:
            step_g(j - 2)
        if 3 <= j:
            step_h(j - 3)
        if level == 3:
            if j == NJ:
                gossip_quarter()
        elif 1 <= j <= 5:
            gossip_half(2 * j - 2)
            gossip_half(2 * j - 1)

    m_load.wait()
    rate = rate_ref[0]
    if level == 3:
        for d in range(1, 4):
            arrived(hb.at[:, part(lax.rem(member + 4 - d, 4))], br.at[d - 1])
    out_copies = []
    for j in range(NJ):
        for t in (j, NJ + j):
            if level != 3:
                arrived(gbuf.at[t], br.at[t])
            arrived(gh.at[t], hsr.at[t])

            @pl.loop(0, 5)
            def _(i, t=t):
                rows = pl.ds(pl.multiple_of(i * 64, 64), 64)
                cols = pl.ds(t * COLS, COLS)
                moved = (0.9 * mom[rows, cols].astype(F32) + gh[t, rows].astype(F32)).astype(BF)
                mom[rows, cols] = moved
                if level == 3:
                    mixed = hb[t, rows].astype(F32)
                else:
                    mixed = (win[t, rows] + gbuf[t, rows].astype(F32)) * 0.5
                win[t, rows] = mixed - rate * moved.astype(F32)

            cols = pl.ds(t * COLS, COLS)
            for copy in (pltpu.make_async_copy(win.at[t], neww_hbm.at[:, cols], outs.at[0, t]),
                         pltpu.make_async_copy(mom.at[:, cols], newm_hbm.at[:, cols], outs.at[1, t])):
                copy.start()
                out_copies.append(copy)

    for away, copy in x_away:
        pl.when(away)(copy.wait_send)
    for j in range(NJ):
        keep, dst, first, second = send_w(j)
        pl.when(jnp.logical_not(home))(first.wait_send)
        second.wait_send()
        first, second = h_copies[j]
        pl.when(jnp.logical_not(home))(first.wait_send)
        second.wait_send()

    @pl.when(jnp.logical_not(home))
    def _():
        t_first.wait_send()
        m_first.wait_send()

    for copy in [t_second, m_second, *relays, *w_on, *p_copies, *r_copies, *g_copies, *a_copies, *b_copies]:
        copy.wait_send()
    for copy in out_copies:
        copy.wait()


def update(level, rate, tokens, goals, marks, shard, momentum):
    dma = pltpu.SemaphoreType.DMA
    anywhere = pl.BlockSpec(memory_space=pl.ANY)
    vm = pltpu.VMEM
    return pl.pallas_call(
        functools.partial(kernel, level),
        out_shape=(
            jax.ShapeDtypeStruct((ROWS, NT * COLS), F32),
            jax.ShapeDtypeStruct((ROWS, NT * COLS), BF),
        ),
        in_specs=[pl.BlockSpec(memory_space=pltpu.SMEM)] + [anywhere] * 5,
        out_specs=(anywhere, anywhere),
        scratch_shapes=[
            vm((NT, ROWS, COLS), F32),
            vm((NT, ROWS, COLS), BF),
            vm((ROWS, NT * COLS), BF),
            vm((4, SEQ, HALF), BF),
            vm((4, HALF, SEQ), BF),
            vm((2 * SEQ, HALF), BF),
            vm((2 * SEQ, 128), BF),
            vm((NJ, HALF, COLS), BF),
            vm((NJ, 4 * SEQ, COLS), F32),
            vm((NJ, 2 * SEQ, COLS), F32),
            vm((NJ, 4 * SEQ, COLS), BF),
            vm((NJ, 2 * ROWS, COLS), BF),
            vm((NJ, 2 * ROWS, COLS), F32),
            vm((NJ, 2 * ROWS, COLS), BF),
            vm((NJ, 2 * ROWS, COLS), BF),
            vm((NT, ROWS, COLS), BF),
            vm((NT, ROWS, COLS), BF),
            vm((NT, ROWS, COLS), BF),
            vm((NT, ROWS, COLS), BF),
            dma((NT + 1,)),
            dma((2,)), dma((2,)),
            dma((2,)), dma((2,)),
            dma((2,)), dma((2,)),
            dma((2,)), dma((2,)),
            dma((2, NJ)), dma((2, NJ)),
            dma((NJ,)), dma((NJ,)),
            dma((NJ,)), dma((NJ,)),
            dma((NJ,)), dma((NJ,)),
            dma((NJ,)), dma((NJ,)),
            dma((2, NJ)), dma((NT,)),
            dma((NT,)), dma((NT,)),
            dma((NT,)), dma((NT,)),
            dma((2, NT)),
        ],
        compiler_params=pltpu.CompilerParams(
            collective_id=level, has_side_effects=True, vmem_limit_bytes=60 * 2**20
        ),
        name=f"update_{level}",
    )(rate, tokens, goals, marks, shard, momentum)


def local(inputs, targets, masked, step_index, weights, momentum):
    marks = jnp.broadcast_to((masked[0].astype(F32) / 2048.0).astype(BF)[:, None], (SEQ, 128))
    rate = ((step_index.astype(F32) + 1.0) / 500.0).reshape(1)
    branches = [functools.partial(update, level) for level in range(5)]
    new_weights, new_momentum = lax.switch(
        step_index % 5, branches, rate, inputs[0], targets[0], marks, weights[0], momentum[0]
    )
    return new_weights[None], new_momentum[None]


def solution(mesh):
    in_specs = (
        P("replica", "fsdp", None),
        P("replica", "fsdp", None),
        P("replica", "fsdp"),
        P(),
        P("replica", "fsdp", None),
        P("replica", "fsdp", None),
    )
    out_specs = (P("replica", "fsdp", None), P("replica", "fsdp", None))
    return jax.shard_map(local, mesh=mesh, in_specs=in_specs, out_specs=out_specs, check_vma=False)
```

time: 389 us -> 157 us (0.40)
  the two profiles are of different devices: /device:TPU:1 before, /device:TPU:6 now
where the time goes in v1:
time: 157 us
  Pallas kernels  150 us (96%)
  local copies, waits for them, and re-layouts  4.48 us (3%)
    pallas_call x1, Pallas kernels, update(): pl.pallas_call(functools.partial(kernel, level), out_shape=(jax.ShapeDtyp...  150 us
    unnamed x4, local copies, waits for them, and re-layouts  3.75 us

profile of v1, /device:TPU:6, one launch (start us, length us, event | category | flops | bytes accessed | tf_op | source)
XLA Modules:
  0.0 156.5 jit_solution(2082245130957085928)
XLA Ops:
  1.3 0.7 convert_bitcast_fusion
  2.0 150.8 %conditional.1 = ((f32[320,2560]{1,0:T(8,128)S(1)}, bf16[320,2560]{1,0:T(8,128)(2,1)})) conditional(s32[]{:T(128)} %clamp.3, (f32[]{:T(128)}, bf16[1,256,2560]{2,1,0:T(8,128)(2,1)}, bf16[1,256,2560]{2,1,0:T(8,128)(2,1)}, bf16[256,1]{0,1:T(2,128)(2,1)S(1)}, f32[1,320,2560]{2,1,0:T(8,128)}, ...), branch_computations={%region_0.1_spmd, %region_1.2_spmd, %region_2.3_spmd, %region_3.4_... | conditional | flops 2 | bytes 67106 | solution.py:424
  2.0 0.7 broadcast_in_dim.75.m_hbm
  2.7 149.7 %update_2.2 = (f32[320,2560]{1,0:T(8,128)S(1)}, bf16[320,2560]{1,0:T(8,128)(2,1)}) custom-call(f32[1]{0:T(128)} %bitcast.10.rate_ref, bf16[256,2560]{1,0:T(8,128)(2,1)} %bitcast.41, bf16[256,2560]{1,0:T(8,128)(2,1)} %bitcast.46, bf16[256,128]{1,0:T(8,128)(2,1)} %broadcast_in_dim.75.m_hbm, f32[320,2560]{1,0:T(8,128)} %bitcast.31, bf16[320,2560]{1,0:T(8,128)(2,1)} %bitcast.36), custom_call_target="tpu_custom_call" | custom-call | tf_op jit(solution)/shard_map/cond/branch_2_fun/update_2/pallas_call | solution.py:370
  152.7 0.0 copy-start
  152.8 1.7 %copy.21 = f32[1,320,2560]{2,1,0:T(8,128)} copy(f32[1,320,2560]{2,1,0:T(8,128)S(1)} %bitcast.49) | data formatting | bytes 6553600
  154.5 0.9 copy-done
  155.3 1.2 copy.22
  (1 shorter events, 0.0 us)
Async XLA Ops:
  152.7 2.6 %copy-start = (bf16[320,2560]{1,0:T(8,128)(2,1)S(1)}, bf16[320,2560]{1,0:T(8,128)(2,1)}, u32[]{:S(2)}) copy-start(bf16[320,2560]{1,0:T(8,128)(2,1)} %get-tuple-element.240) | copy-start | bytes 4915204

commit v2 on v0

v2 whole, which is shorter than its diff:
```python
import functools

import jax
import jax.numpy as jnp
from jax import lax
from jax.experimental import pallas as pl
from jax.experimental.pallas import tpu as pltpu
from jax.sharding import PartitionSpec as P

MESH = pl.DeviceIdType.MESH
BF = jnp.bfloat16
F32 = jnp.float32
COLS = 256
NT = 10
NJ = 5
ROWS = 320
SEQ = 256
HALF = 1280


def span(start, size):
    return pl.ds(pl.multiple_of(start, size), size)


def kernel(level, rate_ref, x_hbm, t_hbm, m_hbm, w_hbm, mom_hbm, neww_hbm, newm_hbm,
           win, wb, mom, xk, xt, tk, mk, wk, ps, pr, rb, gb, go, gr, hs, gh, ga, hb, gbuf,
           ld, xs, xr, xos, xor_, ts, tr, ms, mr, ws, wr, wss, wsr, pss, psr, rs, rr,
           gs, grr, hss, hsr, as_, ar, bs, br, outs):
    r = lax.axis_index("replica")
    f = lax.axis_index("fsdp")
    c = lax.rem(r, 2)
    pair = r - c
    yh = f // 4
    x = lax.rem(f, 4)
    lo = lax.rem(x, 2)
    hi = x // 2
    xo = x + 1 - 2 * lo
    across = 3 - x
    o = lax.rem(lo + hi, 2)
    home = c == yh
    away = jnp.logical_not(home)

    def dev(core, y, xx):
        return (pair + core, y * 4 + xx)

    def other(offset):
        return (lax.rem(r + offset, 32), f)

    partner = dev(1 - c, yh, x)
    worker = dev(yh, c, x)
    worker_o = dev(yh, c, xo)
    side_o = dev(c, yh, xo)
    side_s = dev(c, yh, across)

    def remote(src, dst, ss, rsem, to):
        return pltpu.make_async_remote_copy(src_ref=src, dst_ref=dst, send_sem=ss, recv_sem=rsem,
                                            device_id=to, device_id_type=MESH)

    def arrived(dst, rsem, site=None):
        remote(dst, dst, rsem, rsem, partner).wait_recv()

    def local_or_remote(src, dst, ss, rsem):
        @pl.when(home)
        def _():
            pltpu.make_async_copy(src, dst, rsem).start()

        @pl.when(away)
        def _():
            remote(src, dst, ss, rsem, worker).start()

    def w_load(t):
        return pltpu.make_async_copy(w_hbm.at[:, span(t * COLS, COLS)], win.at[t], ld.at[t])

    @pl.loop(0, NJ)
    def _(j):
        w_load(o * NJ + j).start()

    @pl.loop(0, NJ)
    def _(j):
        w_load((1 - o) * NJ + j).start()

    m_load = pltpu.make_async_copy(mom_hbm, mom, ld.at[NT])
    m_load.start()

    near, later = 2**level, 2 ** ((level + 1) % 5)
    if level == 3:
        offsets = [8, 16, 24]
    else:
        offsets = sorted({near, 32 - near, later, 32 - later})
    barrier = pltpu.get_barrier_semaphore()
    peers = [partner, dev(c, 1 - yh, x), dev(1 - c, 1 - yh, x), side_s]
    peers += [dev(a, b, xo) for a in (0, 1) for b in (0, 1)]
    peers += [other(a) for a in offsets]
    for peer in peers:
        pl.semaphore_signal(barrier, inc=1, device_id=peer, device_id_type=MESH)
    pl.semaphore_wait(barrier, len(peers))

    def x_send(k):
        return remote(x_hbm.at[:, span(k * HALF, HALF)], xk.at[yh * 2 + lo], xs.at[k], xr.at[yh], dev(k, c, x))

    @pl.loop(0, 2)
    def _(k):
        mine = jnp.logical_and(home, c == k)

        @pl.when(mine)
        def _():
            pltpu.make_async_copy(x_hbm.at[:, span(k * HALF, HALF)], xk.at[yh * 2 + lo], xr.at[yh]).start()

        @pl.when(jnp.logical_not(mine))
        def _():
            x_send(k).start()

    def own_rows(j):
        return wk.at[j, span(x * ROWS, ROWS)]

    def o_rows(j):
        return wk.at[j, span(xo * ROWS, ROWS)]

    def w_keep(j):
        return remote(wb.at[o * NJ + j], own_rows(j), ws.at[0, j], wr.at[lo, j], worker)

    def w_give(j):
        return remote(wb.at[(1 - o) * NJ + j], own_rows(j), ws.at[1, j], wr.at[lo, j], worker_o)

    def w_own_on(src, j):
        return remote(src, own_rows(j), wss.at[0, j], wsr.at[lo, j], side_s)

    def w_o_on(j):
        return remote(o_rows(j), o_rows(j), wss.at[1, j], wsr.at[1 - lo, j], side_s)

    def cast(t):
        w_load(t).wait()
        wb[t] = win[t].astype(BF)

    def t_cols(side, j):
        half = o if side == 0 else 1 - o
        return t_hbm.at[:, span(half * HALF + j * COLS, COLS)]

    t_dst = span(lo * SEQ, SEQ)

    def t_keep(j):
        return remote(t_cols(0, j), tk.at[j, t_dst], ts.at[0, j], tr.at[lo, j], worker)

    def t_give(j):
        return remote(t_cols(1, j), tk.at[j, t_dst], ts.at[1, j], tr.at[lo, j], worker_o)

    m_dst = mk.at[span(lo * SEQ, SEQ)]
    m_keep = remote(m_hbm, m_dst, ms.at[0], mr.at[lo], worker)
    m_give = remote(m_hbm, m_dst, ms.at[1], mr.at[lo], worker_o)

    @pl.loop(0, NJ)
    def _(j):
        t = o * NJ + j
        cast(t)

        @pl.when(home)
        def _():
            pltpu.make_async_copy(wb.at[t], own_rows(j), wr.at[lo, j]).start()
            w_own_on(wb.at[t], j).start()
            pltpu.make_async_copy(t_cols(0, j), tk.at[j, t_dst], tr.at[lo, j]).start()

        @pl.when(away)
        def _():
            w_keep(j).start()

    def turn(slot):
        xt[:, span(slot * SEQ, SEQ)] = xk[slot].T

    def x_on(ry):
        slot = ry * 2 + lo
        return remote(xk.at[slot], xk.at[slot], xos.at[ry], xor_.at[ry], side_o)

    arrived(xk.at[yh * 2 + lo], xr.at[yh], 0)
    x_on(yh).start()

    def give(j):
        w_give(j).start()
        t_give(j).start()

        @pl.when(away)
        def _():
            t_keep(j).start()

    cast((1 - o) * NJ)

    @pl.when(home)
    def _():
        give(0)
        m_give.start()
        pltpu.make_async_copy(m_hbm, m_dst, mr.at[lo]).start()

    @pl.loop(1, NJ)
    def _(j):
        cast((1 - o) * NJ + j)

    if level == 3:
        member = r // 8
        quarter = ROWS // 4

        def part(q):
            return span(q * quarter, quarter)

        def a_copy(d):
            q = lax.rem(member + d, 4)
            return remote(wb.at[:, part(q)], ga.at[:, part(d - 1)], as_.at[d - 1], ar.at[d - 1], other(8 * d))

        def b_copy(d):
            return remote(hb.at[:, part(member)], hb.at[:, part(member)], bs.at[d - 1], br.at[d - 1], other(8 * d))

        first_copies, second_copies = (1, 4), (1, 4)
    else:

        def a_copy(t):
            return remote(wb.at[t], ga.at[t], as_.at[t], ar.at[t], other(near))

        def b_copy(t):
            return remote(hb.at[t], gbuf.at[t], bs.at[t], br.at[t], other(later))

        first_copies, second_copies = (0, NT), (0, NT)

    def first_transfer():
        @pl.loop(*first_copies)
        def _(t):
            a_copy(t).start()

    if level >= 2:
        first_transfer()
    turn(yh * 2 + lo)
    arrived(xk.at[(1 - yh) * 2 + lo], xr.at[1 - yh], 1)
    x_on(1 - yh).start()

    @pl.when(home)
    def _():
        pl.loop(1, NJ)(give)

    @pl.when(away)
    def _():
        give(0)
        m_keep.start()
        m_give.start()

    turn((1 - yh) * 2 + lo)

    def gossip_half(t):
        arrived(ga.at[t], ar.at[t], 40 + t)

        @pl.loop(0, 5)
        def _(i):
            rows = span(i * 64, 64)
            half = (win[t, rows] + ga[t, rows].astype(F32)) * 0.5
            win[t, rows] = half
            hb[t, rows] = half.astype(BF)

        b_copy(t).start()

    def gossip_quarter():
        for d in range(3):
            arrived(ga.at[:, part(d)], ar.at[d], 40 + d)

        @pl.loop(0, NT)
        def _(t):
            total = win[t, part(member)]
            for d in range(3):
                total += ga[t, part(d)].astype(F32)
            hb[t, part(member)] = (total * 0.25).astype(BF)

        @pl.loop(*second_copies)
        def _(d):
            b_copy(d).start()

    def forward(j):
        arrived(o_rows(j), wr.at[1 - lo, j], 50 + j)
        w_o_on(j).start()

    @pl.when(away)
    def _():
        @pl.loop(0, NJ)
        def _(j):
            arrived(own_rows(j), wr.at[lo, j], 2)
            w_own_on(own_rows(j), j).start()

        pl.loop(1, NJ)(give)

    arrived(xk.at[yh * 2 + 1 - lo], xor_.at[yh], 3)
    turn(yh * 2 + 1 - lo)
    if level == 2:

        @pl.loop(0, 4)
        def _(t):
            gossip_half(t)

    forward(0)
    arrived(xk.at[(1 - yh) * 2 + 1 - lo], xor_.at[1 - yh], 4)

    def p_copy(j):
        return remote(ps.at[j, span((1 - c) * 512, 512)], pr.at[j], pss.at[j], psr.at[j], partner)

    def step_p(j):
        @pl.when(home)
        def _():
            arrived(own_rows(j), wr.at[lo, j], 5)

        arrived(wk.at[j, span(across * ROWS, ROWS)], wsr.at[1 - lo, j], 60 + j)
        arrived(wk.at[j, span((3 - xo) * ROWS, ROWS)], wsr.at[lo, j], 70 + j)

        @pl.loop(0, 4)
        def _(i):
            b = lax.rem((1 - c) * 2 + i, 4)
            ps[j, span(b * SEQ, SEQ)] = jnp.dot(xk[b], wk[j], preferred_element_type=F32)

            @pl.when(i == 1)
            def _():
                p_copy(j).start()

    def r_copy(j):
        ref = rb.at[j, span(c * 512, 512)]
        return remote(ref, ref, rs.at[j], rr.at[j], partner)

    def step_r(j):
        @pl.when(j == 0)
        def _():
            for side in range(2):
                arrived(mk.at[pl.ds(side * SEQ, SEQ)], mr.at[side], 6)

        arrived(tk.at[j, span(lo * SEQ, SEQ)], tr.at[lo, j], 80 + j)
        arrived(tk.at[j, span((1 - lo) * SEQ, SEQ)], tr.at[1 - lo, j], 80 + j)
        arrived(pr.at[j], psr.at[j], 90 + j)

        @pl.loop(0, 8)
        def _(i):
            rows = span(i * 64, 64)
            full = span(c * 512 + i * 64, 64)
            scale = mk[rows].astype(F32)
            scale = jnp.concatenate([scale, scale], axis=1)
            pred = ps[j, full] + pr[j, rows]
            rb[j, full] = (scale * (pred - tk[j, rows].astype(F32))).astype(BF)

        r_copy(j).start()

    def g_copy(j):
        return remote(gb.at[j], gr.at[j], gs.at[j], grr.at[j], side_s)

    def step_g(j):
        arrived(rb.at[j, span((1 - c) * 512, 512)], rr.at[j], 100 + j)

        @pl.loop(0, 4)
        def _(i):
            half = jnp.where(i < 2, 1 - hi, hi)
            row = half * 2 * ROWS + lax.rem(i, 2) * ROWS
            value = jnp.dot(xt[span(row, ROWS)], rb[j], preferred_element_type=F32)
            rows = span(lax.rem(i, 2) * ROWS, ROWS)

            @pl.when(i < 2)
            def _():
                gb[j, rows] = value.astype(BF)

            @pl.when(i >= 2)
            def _():
                go[j, rows] = value

            @pl.when(i == 1)
            def _():
                g_copy(j).start()

    def h_give(j):
        return remote(hs.at[j, span((1 - lo) * ROWS, ROWS)], gh.at[o * NJ + j], hss.at[1, j], hsr.at[o * NJ + j], worker_o)

    def h_keep(j):
        return remote(hs.at[j, span(lo * ROWS, ROWS)], gh.at[o * NJ + j], hss.at[0, j], hsr.at[o * NJ + j], worker)

    def step_h(j):
        arrived(gr.at[j], grr.at[j], 110 + j)

        @pl.loop(0, 10)
        def _(i):
            rows = span(i * 64, 64)
            hs[j, rows] = (go[j, rows] + gr[j, rows].astype(F32)).astype(BF)

        h_give(j).start()
        local_or_remote(hs.at[j, span(lo * ROWS, ROWS)], gh.at[o * NJ + j], hss.at[0, j], hsr.at[o * NJ + j])

    rate = rate_ref[0]

    def out_w(t):
        return pltpu.make_async_copy(win.at[t], neww_hbm.at[:, span(t * COLS, COLS)], outs.at[0, t])

    def out_m(t):
        cols = span(t * COLS, COLS)
        return pltpu.make_async_copy(mom.at[:, cols], newm_hbm.at[:, cols], outs.at[1, t])

    def finish(t):
        arrived(gh.at[t], hsr.at[t], 120 + t)
        if level != 3:
            arrived(gbuf.at[t], br.at[t], 130 + t)

        @pl.loop(0, 5)
        def _(i):
            rows = span(i * 64, 64)
            cols = span(t * COLS, COLS)
            moved = (0.9 * mom[rows, cols].astype(F32) + gh[t, rows].astype(F32)).astype(BF)
            mom[rows, cols] = moved
            if level == 3:
                mixed = hb[t, rows].astype(F32)
            else:
                mixed = (win[t, rows] + gbuf[t, rows].astype(F32)) * 0.5
            win[t, rows] = mixed - rate * moved.astype(F32)

        out_w(t).start()
        out_m(t).start()

    @pl.loop(0, NJ + 4)
    def _(i):
        @pl.when(i < NJ)
        def _():
            step_p(i)

            @pl.when(i == 0)
            def _():
                turn((1 - yh) * 2 + 1 - lo)
                if level < 2:
                    first_transfer()

            @pl.when(i < NJ - 1)
            def _():
                forward(i + 1)

            step_r(i)
            step_g(i)

        @pl.when(jnp.logical_and(i >= 2, i < NJ + 2))
        def _():
            step_h(i - 2)

        if level == 3:

            @pl.when(i == 1)
            def _():
                gossip_quarter()
        elif level == 2:

            @pl.when(i < 2)
            def _():
                @pl.loop(4 + 3 * i, 7 + 3 * i)
                def _(t):
                    gossip_half(t)
        else:
            lag = 1 if level < 2 else 0

            @pl.when(jnp.logical_and(i >= lag, i < lag + 5))
            def _():
                @pl.loop(2 * (i - lag), 2 * (i - lag) + 2)
                def _(t):
                    gossip_half(t)

        @pl.when(i == 4)
        def _():
            m_load.wait()
            if level == 3:
                for d in range(1, 4):
                    arrived(hb.at[:, part(lax.rem(member + 4 - d, 4))], br.at[d - 1], 130)

        @pl.when(i >= 4)
        def _():
            @pl.loop(0, 2)
            def _(h):
                finish(h * NJ + i - 4)

    @pl.loop(0, 2)
    def _(k):
        @pl.when(jnp.logical_not(jnp.logical_and(home, c == k)))
        def _():
            x_send(k).wait_send()

        x_on(k).wait_send()

    m_give.wait_send()
    pl.when(away)(m_keep.wait_send)

    @pl.loop(0, NJ)
    def _(j):
        @pl.when(away)
        def _():
            w_keep(j).wait_send()
            t_keep(j).wait_send()
            h_keep(j).wait_send()

        for copy in (w_give(j), t_give(j), h_give(j), w_own_on(own_rows(j), j), w_o_on(j), p_copy(j), r_copy(j), g_copy(j)):
            copy.wait_send()

    @pl.loop(*first_copies)
    def _(t):
        a_copy(t).wait_send()

    @pl.loop(*second_copies)
    def _(t):
        b_copy(t).wait_send()

    @pl.loop(0, NT)
    def _(t):
        out_w(t).wait()
        out_m(t).wait()


def update(level, rate, tokens, goals, marks, shard, momentum):
    dma = pltpu.SemaphoreType.DMA
    anywhere = pl.BlockSpec(memory_space=pl.ANY)
    vm = pltpu.VMEM
    return pl.pallas_call(
        functools.partial(kernel, level),
        out_shape=(
            jax.ShapeDtypeStruct((ROWS, NT * COLS), F32),
            jax.ShapeDtypeStruct((ROWS, NT * COLS), BF),
        ),
        in_specs=[pl.BlockSpec(memory_space=pltpu.SMEM)] + [anywhere] * 5,
        out_specs=(anywhere, anywhere),
        scratch_shapes=[
            vm((NT, ROWS, COLS), F32),
            vm((NT, ROWS, COLS), BF),
            vm((ROWS, NT * COLS), BF),
            vm((4, SEQ, HALF), BF),
            vm((HALF, 4 * SEQ), BF),
            vm((NJ, 2 * SEQ, COLS), BF),
            vm((2 * SEQ, 128), BF),
            vm((NJ, HALF, COLS), BF),
            vm((NJ, 4 * SEQ, COLS), F32),
            vm((NJ, 2 * SEQ, COLS), F32),
            vm((NJ, 4 * SEQ, COLS), BF),
            vm((NJ, 2 * ROWS, COLS), BF),
            vm((NJ, 2 * ROWS, COLS), F32),
            vm((NJ, 2 * ROWS, COLS), BF),
            vm((NJ, 2 * ROWS, COLS), BF),
            vm((NT, ROWS, COLS), BF),
            vm((NT, ROWS, COLS), BF),
            vm((NT, ROWS, COLS), BF),
            vm((NT, ROWS, COLS), BF),
            dma((NT + 1,)),
            dma((2,)), dma((2,)),
            dma((2,)), dma((2,)),
            dma((2, NJ)), dma((2, NJ)),
            dma((2,)), dma((2,)),
            dma((2, NJ)), dma((2, NJ)),
            dma((2, NJ)), dma((2, NJ)),
            dma((NJ,)), dma((NJ,)),
            dma((NJ,)), dma((NJ,)),
            dma((NJ,)), dma((NJ,)),
            dma((2, NJ)), dma((NT,)),
            dma((NT,)), dma((NT,)),
            dma((NT,)), dma((NT,)),
            dma((2, NT)),
        ],
        compiler_params=pltpu.CompilerParams(
            collective_id=level, has_side_effects=True, vmem_limit_bytes=60 * 2**20
        ),
        name=f"update_{level}",
    )(rate, tokens, goals, marks, shard, momentum)


def local(inputs, targets, masked, step_index, weights, momentum):
    marks = jnp.broadcast_to((masked[0].astype(F32) / 2048.0).astype(BF)[:, None], (SEQ, 128))
    rate = ((step_index.astype(F32) + 1.0) / 500.0).reshape(1)
    branches = [functools.partial(update, level) for level in range(5)]
    new_weights, new_momentum = lax.switch(
        step_index % 5, branches, rate, inputs[0], targets[0], marks, weights[0], momentum[0]
    )
    return new_weights[None], new_momentum[None]


def solution(mesh):
    in_specs = (
        P("replica", "fsdp", None),
        P("replica", "fsdp", None),
        P("replica", "fsdp"),
        P(),
        P("replica", "fsdp", None),
        P("replica", "fsdp", None),
    )
    out_specs = (P("replica", "fsdp", None), P("replica", "fsdp", None))
    return jax.shard_map(local, mesh=mesh, in_specs=in_specs, out_specs=out_specs, check_vma=False)
```

time: 389 us -> 123 us (0.32)
  waiting for transfers between devices: 304 us -> 0 us
  Pallas kernels: 0 us -> 117 us
  local copies, waits for them, and re-layouts: 39.2 us -> 4.48 us
  matrix products: 14 us -> 0 us
  other arithmetic: 14.5 us -> 0.71 us
  between operations: 14.8 us -> 1.31 us
    all_gather x1 -> x0, waiting for transfers between devices: 161 us -> none  [local(): lax.all_gather(shard.astype(jnp.bfloat16), 'fsdp', axis=0, tiled=True)]
    pallas_call x0 -> x1, Pallas kernels: none -> 117 us  [update(): pl.pallas_call(functools.partial(kernel, level), out_shape=(jax.ShapeDtyp...]
    ppermute x2 -> x0, waiting for transfers between devices: 111 us -> none  [passed_along(): lax.ppermute(x, axis, [(i, (i + by) % length) for i in range(length)])]
    unnamed x3 -> x0, waiting for transfers between devices: 32.2 us -> none
    unnamed x15 -> x4, local copies, waits for them, and re-layouts: 33.7 us -> 3.75 us
    dot_general x1 -> x0, matrix products: 14 us -> none  [local(): lax.dot_general(columns, resid, (((0,), (0,)), ((), ())), preferred_eleme...]
    broadcast_in_dim x1 -> x0, other arithmetic: 6.01 us -> none  [local(): return (new_weights[None], new_momentum[None])]
    cond x3 -> x0, local copies, waits for them, and re-layouts: 5.49 us -> none  [the longest x1 5.48 us: local(): mixed = lax.switch(step_index % levels, branches, shard)]
  transfers between devices with their start and end apart: 4 -> 0, of which waited for: 4 -> 0; matrix products, arithmetic and copies ran while one was open for 4% -> 0% of each run, Pallas kernels for 0% -> 0%
where the time goes in v2:
time: 123 us
  Pallas kernels  117 us (95%)
  local copies, waits for them, and re-layouts  4.48 us (4%)
  between operations  1.31 us (1%)
    pallas_call x1, Pallas kernels, update(): pl.pallas_call(functools.partial(kernel, level), out_shape=(jax.ShapeDtyp...  117 us
    unnamed x4, local copies, waits for them, and re-layouts  3.75 us

profile of v2, /device:TPU:1, one launch (start us, length us, event | category | flops | bytes accessed | tf_op | source)
XLA Modules:
  0.0 123.3 jit_solution(573075919435630234)
XLA Ops:
  1.3 0.7 convert_bitcast_fusion
  2.0 117.5 %conditional.1 = ((f32[320,2560]{1,0:T(8,128)S(1)}, bf16[320,2560]{1,0:T(8,128)(2,1)})) conditional(s32[]{:T(128)} %clamp.3, (f32[]{:T(128)}, bf16[1,256,2560]{2,1,0:T(8,128)(2,1)}, bf16[1,256,2560]{2,1,0:T(8,128)(2,1)}, bf16[256,1]{0,1:T(2,128)(2,1)S(1)}, f32[1,320,2560]{2,1,0:T(8,128)}, ...), branch_computations={%region_0.1_spmd, %region_1.2_spmd, %region_2.3_spmd, %region_3.4_... | conditional | flops 2 | bytes 67106 | solution.py:562
  2.0 0.7 broadcast_in_dim.79.m_hbm
  2.7 116.7 %update_3.2 = (f32[320,2560]{1,0:T(8,128)S(1)}, bf16[320,2560]{1,0:T(8,128)(2,1)}) custom-call(f32[1]{0:T(128)} %bitcast.15.rate_ref, bf16[256,2560]{1,0:T(8,128)(2,1)} %bitcast.42, bf16[256,2560]{1,0:T(8,128)(2,1)} %bitcast.47, bf16[256,128]{1,0:T(8,128)(2,1)} %broadcast_in_dim.79.m_hbm, f32[320,2560]{1,0:T(8,128)} %bitcast.32, bf16[320,2560]{1,0:T(8,128)(2,1)} %bitcast.37), custom_call_target="tpu_custom_call" | custom-call | tf_op jit(solution)/shard_map/cond/branch_3_fun/update_3/pallas_call | solution.py:508
  119.5 0.0 copy-start
  119.5 1.7 %copy.21 = f32[1,320,2560]{2,1,0:T(8,128)} copy(f32[1,320,2560]{2,1,0:T(8,128)S(1)} %bitcast.49) | data formatting | bytes 6553600
  121.2 0.9 copy-done
  122.1 1.2 copy.22
  (1 shorter events, 0.0 us)
Async XLA Ops:
  119.5 2.6 %copy-start = (bf16[320,2560]{1,0:T(8,128)(2,1)S(1)}, bf16[320,2560]{1,0:T(8,128)(2,1)}, u32[]{:S(2)}) copy-start(bf16[320,2560]{1,0:T(8,128)(2,1)} %get-tuple-element.240) | copy-start | bytes 4915204

commit v3 on v2

--- a/solution.py
+++ b/solution.py
@@ -23,7 +23,7 @@
 
 
 def kernel(level, rate_ref, x_hbm, t_hbm, m_hbm, w_hbm, mom_hbm, neww_hbm, newm_hbm,
-           win, wb, mom, xk, xt, tk, mk, wk, ps, pr, rb, gb, go, gr, hs, gh, ga, hb, gbuf,
+           win, wb, mom, xk, xt, tk, mk, wk, ps, pr, rb, gb, go, gr, hs, gh, ga, hb, gbuf, rel,
            ld, xs, xr, xos, xor_, ts, tr, ms, mr, ws, wr, wss, wsr, pss, psr, rs, rr,
            gs, grr, hss, hsr, as_, ar, bs, br, outs):
     r = lax.axis_index("replica")
@@ -83,10 +83,16 @@
     m_load.start()
 
     near, later = 2**level, 2 ** ((level + 1) % 5)
+    if level == 1:
+        near, later = later, near
     if level == 3:
         offsets = [8, 16, 24]
+    elif level == 0:
+        offsets = [1, 2, 3, 29, 30, 31]
     else:
         offsets = sorted({near, 32 - near, later, 32 - later})
+    if level == 2:
+        offsets += [12, 20]
     barrier = pltpu.get_barrier_semaphore()
     peers = [partner, dev(c, 1 - yh, x), dev(1 - c, 1 - yh, x), side_s]
     peers += [dev(a, b, xo) for a in (0, 1) for b in (0, 1)]
@@ -173,20 +179,29 @@
     arrived(xk.at[yh * 2 + lo], xr.at[yh], 0)
     x_on(yh).start()
 
+    def give_t(j):
+        t_give(j).start()
+
+        @pl.when(away)
+        def _():
+            t_keep(j).start()
+
     def give(j):
-        w_give(j).start()
-        t_give(j).start()
-
-        @pl.when(away)
-        def _():
-            t_keep(j).start()
+        @pl.when(j < NJ)
+        def _():
+            w_give(j).start()
+
+        @pl.when(j >= 2)
+        def _():
+            give_t(j - 1)
 
     cast((1 - o) * NJ)
 
     @pl.when(home)
     def _():
-        give(0)
+        w_give(0).start()
         m_give.start()
+        give_t(0)
         pltpu.make_async_copy(m_hbm, m_dst, mr.at[lo]).start()
 
     @pl.loop(1, NJ)
@@ -209,39 +224,53 @@
 
         first_copies, second_copies = (1, 4), (1, 4)
     else:
+        first = 1 + 2 * c if level == 0 else near
 
         def a_copy(t):
-            return remote(wb.at[t], ga.at[t], as_.at[t], ar.at[t], other(near))
+            return remote(wb.at[t], ga.at[t], as_.at[t], ar.at[t], other(first))
+
+        def pass_on(t):
+            return remote(gbuf.at[t], gbuf.at[t], as_.at[NT + t], br.at[t], partner)
 
         def b_copy(t):
             return remote(hb.at[t], gbuf.at[t], bs.at[t], br.at[t], other(later))
 
+        def leg(k):
+            return remote(hb.at[k * NJ], rel.at[k], bs.at[k * NJ], ar.at[NT + k], other(20))
+
+        def next_leg(k):
+            return remote(rel.at[k], gbuf.at[k * NJ], as_.at[NT + k], br.at[k * NJ], other(20))
+
         first_copies, second_copies = (0, NT), (0, NT)
+
+    def order(t):
+        return lax.rem(t, 2) * NJ + t // 2
 
     def first_transfer():
         @pl.loop(*first_copies)
         def _(t):
-            a_copy(t).start()
-
-    if level >= 2:
-        first_transfer()
+            a_copy(t if level == 3 else order(t)).start()
+
+    first_transfer()
     turn(yh * 2 + lo)
     arrived(xk.at[(1 - yh) * 2 + lo], xr.at[1 - yh], 1)
     x_on(1 - yh).start()
 
     @pl.when(home)
     def _():
-        pl.loop(1, NJ)(give)
+        pl.loop(1, NJ + 1)(give)
 
     @pl.when(away)
     def _():
-        give(0)
+        w_give(0).start()
+        give_t(0)
         m_keep.start()
         m_give.start()
 
     turn((1 - yh) * 2 + lo)
 
-    def gossip_half(t):
+    def gossip_half(n):
+        t = order(n)
         arrived(ga.at[t], ar.at[t], 40 + t)
 
         @pl.loop(0, 5)
@@ -251,7 +280,15 @@
             win[t, rows] = half
             hb[t, rows] = half.astype(BF)
 
-        b_copy(t).start()
+        if level == 0:
+            pl.when(c == 1)(b_copy(t).start)
+        elif level == 1:
+            pl.when(n >= 4)(b_copy(t).start)
+        elif level == 2:
+            pl.when(n < 2)(leg(lax.min(n, 1)).start)
+            pl.when(n >= 2)(b_copy(t).start)
+        else:
+            b_copy(t).start()
 
     def gossip_quarter():
         for d in range(3):
@@ -279,11 +316,11 @@
             arrived(own_rows(j), wr.at[lo, j], 2)
             w_own_on(own_rows(j), j).start()
 
-        pl.loop(1, NJ)(give)
+        pl.loop(1, NJ + 1)(give)
 
     arrived(xk.at[yh * 2 + 1 - lo], xor_.at[yh], 3)
     turn(yh * 2 + 1 - lo)
-    if level == 2:
+    if level in (1, 2):
 
         @pl.loop(0, 4)
         def _(t):
@@ -337,8 +374,9 @@
 
         r_copy(j).start()
 
-    def g_copy(j):
-        return remote(gb.at[j], gr.at[j], gs.at[j], grr.at[j], side_s)
+    def g_copy(j, side):
+        rows = span(side * ROWS, ROWS)
+        return remote(gb.at[j, rows], gr.at[j, rows], gs.at[side, j], grr.at[side, j], side_s)
 
     def step_g(j):
         arrived(rb.at[j, span((1 - c) * 512, 512)], rr.at[j], 100 + j)
@@ -346,21 +384,18 @@
         @pl.loop(0, 4)
         def _(i):
             half = jnp.where(i < 2, 1 - hi, hi)
-            row = half * 2 * ROWS + lax.rem(i, 2) * ROWS
-            value = jnp.dot(xt[span(row, ROWS)], rb[j], preferred_element_type=F32)
-            rows = span(lax.rem(i, 2) * ROWS, ROWS)
+            side = lax.rem(lo + i, 2)
+            value = jnp.dot(xt[span((half * 2 + side) * ROWS, ROWS)], rb[j], preferred_element_type=F32)
+            rows = span(side * ROWS, ROWS)
 
             @pl.when(i < 2)
             def _():
                 gb[j, rows] = value.astype(BF)
+                pl.when(away)(g_copy(j, side).start)
 
             @pl.when(i >= 2)
             def _():
                 go[j, rows] = value
-
-            @pl.when(i == 1)
-            def _():
-                g_copy(j).start()
 
     def h_give(j):
         return remote(hs.at[j, span((1 - lo) * ROWS, ROWS)], gh.at[o * NJ + j], hss.at[1, j], hsr.at[o * NJ + j], worker_o)
@@ -369,14 +404,20 @@
         return remote(hs.at[j, span(lo * ROWS, ROWS)], gh.at[o * NJ + j], hss.at[0, j], hsr.at[o * NJ + j], worker)
 
     def step_h(j):
-        arrived(gr.at[j], grr.at[j], 110 + j)
-
-        @pl.loop(0, 10)
+        @pl.loop(0, 2)
         def _(i):
-            rows = span(i * 64, 64)
-            hs[j, rows] = (go[j, rows] + gr[j, rows].astype(F32)).astype(BF)
-
-        h_give(j).start()
+            side = lax.rem(1 - lo + i, 2)
+            arrived(gr.at[j, span(side * ROWS, ROWS)], grr.at[side, j], 110 + j)
+
+            @pl.loop(0, 5)
+            def _(k):
+                rows = span(side * ROWS + k * 64, 64)
+                hs[j, rows] = (go[j, rows] + gr[j, rows].astype(F32)).astype(BF)
+
+            @pl.when(i == 0)
+            def _():
+                h_give(j).start()
+
         local_or_remote(hs.at[j, span(lo * ROWS, ROWS)], gh.at[o * NJ + j], hss.at[0, j], hsr.at[o * NJ + j])
 
     rate = rate_ref[0]
@@ -390,7 +431,9 @@
 
     def finish(t):
         arrived(gh.at[t], hsr.at[t], 120 + t)
-        if level != 3:
+        if level == 0:
+            pl.when(c == 0)(functools.partial(arrived, gbuf.at[t], br.at[t], 130))
+        elif level != 3:
             arrived(gbuf.at[t], br.at[t], 130 + t)
 
         @pl.loop(0, 5)
@@ -410,21 +453,33 @@
 
     @pl.loop(0, NJ + 4)
     def _(i):
+        pl.when(i < NJ)(functools.partial(step_p, i))
+
+        @pl.when(jnp.logical_and(home, jnp.logical_and(i >= 1, i <= NJ)))
+        def _():
+            g_copy(i - 1, lo).start()
+            g_copy(i - 1, 1 - lo).start()
+
         @pl.when(i < NJ)
         def _():
-            step_p(i)
 
             @pl.when(i == 0)
             def _():
                 turn((1 - yh) * 2 + 1 - lo)
-                if level < 2:
-                    first_transfer()
-
-            @pl.when(i < NJ - 1)
-            def _():
-                forward(i + 1)
+                if level == 1:
+
+                    @pl.loop(0, 4)
+                    def _(t):
+                        b_copy(order(t)).start()
+
+                forward(1)
 
             step_r(i)
+
+            @pl.when(i < NJ - 2)
+            def _():
+                forward(i + 2)
+
             step_g(i)
 
         @pl.when(jnp.logical_and(i >= 2, i < NJ + 2))
@@ -436,19 +491,40 @@
             @pl.when(i == 1)
             def _():
                 gossip_quarter()
-        elif level == 2:
+        elif level == 0:
+
+            @pl.when(i < 2)
+            def _():
+                @pl.loop(5 * i, 5 * i + 5)
+                def _(t):
+                    gossip_half(t)
+
+            @pl.when(jnp.logical_and(i == 3, c == 1))
+            def _():
+                @pl.loop(0, NT)
+                def _(t):
+                    arrived(gbuf.at[t], br.at[t], 140)
+                    pass_on(t).start()
+        elif level in (1, 2):
 
             @pl.when(i < 2)
             def _():
                 @pl.loop(4 + 3 * i, 7 + 3 * i)
                 def _(t):
                     gossip_half(t)
+
+            if level == 2:
+
+                @pl.when(i == 2)
+                def _():
+                    for k in range(2):
+                        arrived(rel.at[k], ar.at[NT + k], 141 + k)
+                        next_leg(k).start()
         else:
-            lag = 1 if level < 2 else 0
-
-            @pl.when(jnp.logical_and(i >= lag, i < lag + 5))
-            def _():
-                @pl.loop(2 * (i - lag), 2 * (i - lag) + 2)
+
+            @pl.when(i < 5)
+            def _():
+                @pl.loop(2 * i, 2 * i + 2)
                 def _(t):
                     gossip_half(t)
 
@@ -484,16 +560,31 @@
             t_keep(j).wait_send()
             h_keep(j).wait_send()
 
-        for copy in (w_give(j), t_give(j), h_give(j), w_own_on(own_rows(j), j), w_o_on(j), p_copy(j), r_copy(j), g_copy(j)):
+        for copy in (w_give(j), t_give(j), h_give(j), w_own_on(own_rows(j), j), w_o_on(j), p_copy(j), r_copy(j),
+                     g_copy(j, 0), g_copy(j, 1)):
             copy.wait_send()
 
     @pl.loop(*first_copies)
     def _(t):
         a_copy(t).wait_send()
 
-    @pl.loop(*second_copies)
-    def _(t):
-        b_copy(t).wait_send()
+    if level == 0:
+
+        @pl.when(c == 1)
+        def _():
+            @pl.loop(0, NT)
+            def _(t):
+                b_copy(t).wait_send()
+                pass_on(t).wait_send()
+    else:
+
+        @pl.loop(*second_copies)
+        def _(t):
+            b_copy(t).wait_send()
+
+        if level == 2:
+            for k in range(2):
+                next_leg(k).wait_send()
 
     @pl.loop(0, NT)
     def _(t):
@@ -533,6 +624,7 @@
             vm((NT, ROWS, COLS), BF),
             vm((NT, ROWS, COLS), BF),
             vm((NT, ROWS, COLS), BF),
+            vm((2, ROWS, COLS), BF),
             dma((NT + 1,)),
             dma((2,)), dma((2,)),
             dma((2,)), dma((2,)),
@@ -542,9 +634,9 @@
             dma((2, NJ)), dma((2, NJ)),
             dma((NJ,)), dma((NJ,)),
             dma((NJ,)), dma((NJ,)),
-            dma((NJ,)), dma((NJ,)),
+            dma((2, NJ)), dma((2, NJ)),
             dma((2, NJ)), dma((NT,)),
-            dma((NT,)), dma((NT,)),
+            dma((2 * NT,)), dma((2 * NT,)),
             dma((NT,)), dma((NT,)),
             dma((2, NT)),
         ],

time: 123 us -> 121 us (0.984)
  Pallas kernels: 117 us -> 114 us
    pallas_call x1, Pallas kernels: 117 us -> 114 us  [update(): pl.pallas_call(functools.partial(kernel, level), out_shape=(jax.ShapeDtyp...]
where the time goes in v3:
time: 121 us
  Pallas kernels  114 us (94%)
  local copies, waits for them, and re-layouts  4.48 us (4%)
  between operations  1.31 us (1%)
    pallas_call x1, Pallas kernels, update(): pl.pallas_call(functools.partial(kernel, level), out_shape=(jax.ShapeDtyp...  114 us
    unnamed x4, local copies, waits for them, and re-layouts  3.75 us

profile of v3, /device:TPU:1, one launch (start us, length us, event | category | flops | bytes accessed | tf_op | source)
XLA Modules:
  0.0 120.8 jit_solution(12314344599907587944)
XLA Ops:
  1.3 0.7 convert_bitcast_fusion
  2.0 115.0 %conditional.1 = ((f32[320,2560]{1,0:T(8,128)S(1)}, bf16[320,2560]{1,0:T(8,128)(2,1)})) conditional(s32[]{:T(128)} %clamp.3, (f32[]{:T(128)}, bf16[1,256,2560]{2,1,0:T(8,128)(2,1)}, bf16[1,256,2560]{2,1,0:T(8,128)(2,1)}, bf16[256,1]{0,1:T(2,128)(2,1)S(1)}, f32[1,320,2560]{2,1,0:T(8,128)}, ...), branch_computations={%region_0.1_spmd, %region_1.2_spmd, %region_2.3_spmd, %region_3.4_... | conditional | flops 2 | bytes 67106 | solution.py:654
  2.0 0.7 broadcast_in_dim.67.m_hbm
  2.7 114.2 %update_0.2 = (f32[320,2560]{1,0:T(8,128)S(1)}, bf16[320,2560]{1,0:T(8,128)(2,1)}) custom-call(f32[1]{0:T(128)} %bitcast.rate_ref, bf16[256,2560]{1,0:T(8,128)(2,1)} %bitcast.39, bf16[256,2560]{1,0:T(8,128)(2,1)} %bitcast.44, bf16[256,128]{1,0:T(8,128)(2,1)} %broadcast_in_dim.67.m_hbm, f32[320,2560]{1,0:T(8,128)} %bitcast.29, bf16[320,2560]{1,0:T(8,128)(2,1)} %bitcast.34), custom_call_target="tpu_custom_call" | custom-call | tf_op jit(solution)/shard_map/cond/branch_0_fun/update_0/pallas_call | solution.py:599
  117.0 0.0 copy-start
  117.0 1.7 %copy.21 = f32[1,320,2560]{2,1,0:T(8,128)} copy(f32[1,320,2560]{2,1,0:T(8,128)S(1)} %bitcast.49) | data formatting | bytes 6553600
  118.7 0.9 copy-done
  119.6 1.2 copy.22
  (1 shorter events, 0.0 us)
Async XLA Ops:
  117.0 2.6 %copy-start = (bf16[320,2560]{1,0:T(8,128)(2,1)S(1)}, bf16[320,2560]{1,0:T(8,128)(2,1)}, u32[]{:S(2)}) copy-start(bf16[320,2560]{1,0:T(8,128)(2,1)} %get-tuple-element.240) | copy-start | bytes 4915204
